TPU v7x, 32 devices: a whole 2x2x4 slice. The times are simulated.
32 devices in a mesh: freq: 8 (over z, x), bl: 4 (over y, core).
Axes of the slice: x: 2, y: 2, z: 4, core: 2. Of those that a mesh axis runs over, the one named last changes fastest.
Arguments:
- voltages: bfloat16 [1024, 134144], P(('bl', 'freq')), may hold values from -6 to 6
- fir_taps: float32 [4, 1024], replicated, may hold values from -3 to 3
- antenna_order: int32 [1024], replicated, may hold values from 0 to 1023, each once
- tile_list: int32 [4, 2], replicated, may hold values from 0 to 3
Outputs:
- visibilities: bfloat16 [4, 512, 256, 512], P('bl', 'freq')
All inputs are finite; a program needn't handle non-finite values.
Results may differ from a plain program's by a relative error of at most 0.0074.
Values may be sent and summed in bfloat16 or wider, within the bound.
A program may use at most 128 MiB of HBM per device.

v0:
```python
import math
import jax
import jax.numpy as jnp
from jax import lax
from jax.sharding import PartitionSpec as P

K = 1024
TAPS = 4
PANEL = 256
SAMPLES = 128


def make_table(points, kept):
    product = (
        jnp.arange(points, dtype=jnp.int32)[:, None]
        * jnp.arange(kept, dtype=jnp.int32)[None, :]
        % points
    )
    phase = 2.0 * math.pi / points * product.astype(jnp.float32)
    return jnp.concatenate([jnp.cos(phase), -jnp.sin(phase)], axis=1).astype(jnp.bfloat16)


def arrange(panel):
    width = panel.shape[1]
    return jnp.transpose(panel, (3, 0, 2, 1)).reshape(panel.shape[3], panel.shape[0], 2 * width)


def rotated(panel):
    turned = jnp.stack([-panel[:, :, 1, :], panel[:, :, 0, :]], axis=2)
    return arrange(turned)


def correlate(source, antenna_order, tile):
    row_ids = lax.dynamic_slice_in_dim(antenna_order, tile[0] * PANEL, PANEL)
    col_ids = lax.dynamic_slice_in_dim(antenna_order, tile[1] * PANEL, PANEL)
    row_panel = jnp.take(source, row_ids, axis=0)
    col_panel = jnp.take(source, col_ids, axis=0)
    left = arrange(row_panel)
    right = jnp.concatenate([arrange(col_panel), rotated(col_panel)], axis=1)
    return jnp.einsum("fps,fqs->fpq", left, right, preferred_element_type=jnp.float32)


def per_device(voltages, fir_taps, antenna_order, tile_list):
    local_count = voltages.shape[0]
    frames = voltages.reshape(local_count, SAMPLES + TAPS - 1, K)
    filtered = jnp.zeros((local_count, SAMPLES, K), jnp.float32)
    for tap in range(TAPS):
        filtered = filtered + fir_taps[tap][None, None, :] * frames[
            :, tap : tap + SAMPLES, :
        ].astype(jnp.float32)
    filtered = filtered.astype(jnp.bfloat16)
    table = make_table(K, K // 2)
    spectra = jnp.dot(
        filtered.reshape(local_count * SAMPLES, K), table, preferred_element_type=jnp.float32
    )
    spectra = (
        (spectra * (1.0 / math.sqrt(K)))
        .astype(jnp.bfloat16)
        .reshape(local_count, SAMPLES, 2, K // 2)
    )
    turned = lax.all_to_all(spectra, "freq", split_axis=3, concat_axis=0, tiled=True)
    gathered = lax.all_gather(turned, "bl", axis=0, tiled=True)
    own_tile = tile_list[lax.axis_index("bl")]
    summed = correlate(gathered, antenna_order, own_tile)
    return (summed / SAMPLES).astype(jnp.bfloat16)[None]


def solution(mesh):
    return jax.shard_map(
        per_device,
        mesh=mesh,
        in_specs=(P(("bl", "freq"), None), P(), P(), P()),
        out_specs=P("bl", "freq", None, None),
        check_vma=False,
    )
```

profile of v0, /device:TPU:0, one launch (start us, length us, event | category | flops | bytes accessed | tf_op | source)
XLA Modules:
  0.0 656.6 jit_solution(10840728497448380260)
XLA Ops:
  6.5 0.0 copy-start
  6.5 0.0 all-gather.2.cloned.1.call-start
  6.5 8.5 %negate_convert_fusion = (bf16[1024,512]{1,0:T(8,128)(2,1)S(1)}, bf16[1024,512]{1,0:T(8,128)(2,1)S(1)}) fusion(), kind=kLoop, calls=%fused_computation.23 | loop fusion | flops 8912896 | bytes 2097152 | tf_op jit(solution)/shard_map/convert.1
  15.1 0.0 copy-start.2
  15.1 9.2 %reshape.35 = bf16[32,131,1024]{2,1,0:T(8,128)(2,1)} reshape(bf16[32,134144]{1,0:T(8,128)(2,1)} %param.6) | data formatting | bytes 17170432 | tf_op jit(solution)/shard_map/reshape | solution.py:45
  24.3 0.0 copy-done.2
  24.3 19.3 %add_convert_fusion = bf16[32,128,1024]{2,1,0:T(8,128)(2,1)S(1)} fusion(bf16[32,131,1024]{2,1,0:T(8,128)(2,1)} %reshape.35, f32[1024]{0:T(1024)S(1)} %bitcast.28, f32[1024]{0:T(1024)S(1)} %bitcast.29, f32[1024]{0:T(1024)S(1)} %bitcast.27, f32[1024]{0:T(1024)S(1)} %bitcast.26), kind=kLoop, calls=%fused_computation.9 | loop fusion | flops 50331648 | bytes 41959424 | tf_op jit(solution)/shard_map/convert_element_type | solution.py:51
  43.6 11.0 %multiply_convert_fusion.1 = bf16[4096,1024]{1,0:T(8,128)(2,1)} fusion(bf16[4096,1024]{1,0:T(8,128)(2,1)S(1)} %bitcast.24, bf16[1024,512]{1,0:T(8,128)(2,1)S(1)} %get-tuple-element.20, bf16[1024,512]{1,0:T(8,128)(2,1)S(1)} %get-tuple-element.21), kind=kOutput, calls=%fused_computation.8 | convolution fusion | flops 8602517504 | bytes 18874368 | tf_op jit(solution)/shard_map/dot_general | solution.py:53
  54.6 14.5 %reshape.37 = bf16[32,128,2,512]{3,2,1,0:T(2,128)(2,1)} reshape(bf16[4096,1024]{1,0:T(8,128)(2,1)} %multiply_convert_fusion.1) | data formatting | bytes 16777216 | tf_op jit(solution)/shard_map/reshape | solution.py:59
  69.1 28.1 %copy.15 = bf16[32,128,2,512]{1,2,0,3:T(2,128)(2,1)} copy(bf16[32,128,2,512]{3,2,1,0:T(2,128)(2,1)} %reshape.37) | data formatting | bytes 16777216 | tf_op jit(solution)/shard_map/reshape | solution.py:59
  97.2 190.4 %all_to_all.18 = bf16[32,128,2,512]{1,2,0,3:T(2,128)(2,1)} all-to-all(bf16[32,128,2,512]{1,2,0,3:T(2,128)(2,1)} %copy.15), channel_id=1, replica_groups=mesh['freq'=8,'bl'=4] {'freq'}, dimensions={3} | all-to-all | bytes 16777216 | tf_op jit(solution)/shard_map/all_to_all | solution.py:61
  287.6 16.5 %copy.16 = bf16[32,128,2,512]{1,3,2,0:T(8,128)(2,1)} copy(bf16[32,128,2,512]{1,2,0,3:T(2,128)(2,1)} %all_to_all.18) | data formatting | bytes 16777216 | tf_op jit(solution)/shard_map/all_to_all | solution.py:61
  304.1 9.8 %copy.17 = bf16[8,32,128,2,64]{2,4,3,1,0:T(8,128)(2,1)} copy(bf16[8,32,128,2,64]{2,4,0,3,1:T(8,128)(2,1)} %bitcast.23) | data formatting | bytes 16777216 | tf_op jit(solution)/shard_map/all_to_all | solution.py:61
  313.9 0.0 copy-start.3
  313.9 0.0 all-gather.2.cloned.1.call-update
  313.9 0.0 copy-done
  313.9 0.1 constant_dynamic-slice_fusion
  314.0 0.5 fusion.19
  315.8 0.0 copy-done.3
  315.8 0.1 compare_and_fusion
  315.9 198.8 %all-gather.2.cloned.1.call-done = bf16[1024,128,2,64]{1,3,2,0:T(8,128)(2,1)} async-done(((bf16[256,128,2,64]{1,3,2,0:T(8,128)(2,1)}), bf16[1024,128,2,64]{1,3,2,0:T(8,128)(2,1)}) %all-gather.2.cloned.1.call-update) | async-done | bytes 33554448 | tf_op jit(solution)/shard_map/all_gather | solution.py:62
  514.7 9.1 %gather_fusion.1 = bf16[256,128,2,64]{1,3,2,0:T(8,128)(2,1)} fusion(bf16[1024,128,2,64]{1,3,2,0:T(8,128)(2,1)} %all-gather.2.cloned.1.call-done, s32[1024]{0:T(1024)S(1)} %get-tuple-element.22), kind=kCustom, calls=%fused_computation.1.clone | custom fusion | bytes 16778240 | tf_op jit(solution)/shard_map/jit(_take)/gather | solution.py:37
  523.8 7.4 %broadcast_select_fusion = bf16[256,128,2,64]{1,3,2,0:T(8,128)(2,1)} fusion(bf16[256,128,2,64]{1,3,2,0:T(8,128)(2,1)} %gather_fusion.1, pred[256]{0:T(512)(128)(4,1)S(1)} %get-tuple-element.6), kind=kLoop, calls=%fused_computation.12 | loop fusion | flops 4194304 | bytes 16777472 | tf_op jit(solution)/shard_map/jit(_take)/select_n | solution.py:37
  531.3 7.4 %fusion.22 = bf16[64,256,2,128]{3,0,2,1:T(8,128)(2,1)} fusion(bf16[256,128,2,64]{1,3,2,0:T(8,128)(2,1)} %gather_fusion.1, pred[256]{0:T(512)(128)(4,1)S(1)} %get-tuple-element.6), kind=kLoop, calls=%fused_computation.39 | loop fusion | flops 4194304 | bytes 16777472 | tf_op jit(solution)/shard_map/transpose | solution.py:25
  538.7 9.1 %gather_fusion = bf16[256,128,2,64]{1,3,2,0:T(8,128)(2,1)} fusion(bf16[1024,128,2,64]{1,3,2,0:T(8,128)(2,1)} %all-gather.2.cloned.1.call-done, s32[1024]{0:T(1024)S(1)} %get-tuple-element.23), kind=kCustom, calls=%fused_computation.clone | custom fusion | bytes 16778240 | tf_op jit(solution)/shard_map/jit(_take)/gather | solution.py:36
  547.8 7.6 %select_bitcast_fusion = bf16[64,256,2,128]{3,0,2,1:T(8,128)(2,1)} fusion(bf16[256,128,2,64]{1,3,2,0:T(8,128)(2,1)} %gather_fusion, pred[256]{0:T(512)(128)(4,1)S(1)} %get-tuple-element.16), kind=kLoop, calls=%fused_computation.11 | loop fusion | flops 4194304 | bytes 16777472 | tf_op jit(solution)/shard_map/transpose | solution.py:25
  555.4 12.9 %copy.18 = bf16[64,256,2,128]{1,3,2,0:T(8,128)(2,1)} copy(bf16[64,256,2,128]{3,0,2,1:T(8,128)(2,1)} %select_bitcast_fusion) | data formatting | bytes 16777216 | tf_op jit(solution)/shard_map/transpose | solution.py:25
  568.3 5.2 slice_negate_fusion
  573.6 6.5 maximum_bitcast_fusion
  580.0 13.2 %copy.20 = bf16[64,256,2,128]{3,2,1,0:T(2,128)(2,1)} copy(bf16[64,256,2,128]{3,0,2,1:T(8,128)(2,1)} %maximum_bitcast_fusion) | data formatting | bytes 16777216 | tf_op jit(solution)/shard_map/transpose | solution.py:25
  593.2 14.1 %reshape.40 = bf16[64,256,256]{2,1,0:T(8,128)(2,1)} reshape(bf16[64,256,2,128]{3,2,1,0:T(2,128)(2,1)} %copy.20) | data formatting | bytes 16777216 | tf_op jit(solution)/shard_map/reshape | solution.py:25
  607.3 13.2 %copy.19 = bf16[64,256,2,128]{3,2,1,0:T(2,128)(2,1)} copy(bf16[64,256,2,128]{3,0,2,1:T(8,128)(2,1)} %fusion.22) | data formatting | bytes 16777216 | tf_op jit(solution)/shard_map/transpose | solution.py:25
  620.4 14.1 %reshape.39 = bf16[64,256,256]{2,1,0:T(8,128)(2,1)} reshape(bf16[64,256,2,128]{3,2,1,0:T(2,128)(2,1)} %copy.19) | data formatting | bytes 16777216 | tf_op jit(solution)/shard_map/reshape | solution.py:25
  634.5 0.0 copy-start.1
  634.5 15.2 %fusion = bf16[1,64,256,512]{3,2,1,0:T(8,128)(2,1)} fusion(bf16[64,256,256]{1,2,0:T(8,128)(2,1)} %bitcast.25, bf16[64,256,256]{2,1,0:T(8,128)(2,1)} %reshape.40, bf16[64,256,256]{2,1,0:T(8,128)(2,1)} %reshape.39), kind=kOutput, calls=%fused_computation.3 | convolution fusion | flops 4345298944 | bytes 41943040 | tf_op jit(solution)/shard_map/fps,fqs->fpq/dot_general | solution.py:40
  649.8 0.0 copy-done.1
  (2 shorter events, 0.0 us)
Async XLA Ops:
  6.5 307.4 %copy-start = (s32[4,2]{0,1:T(2,128)S(1)}, s32[4,2]{0,1:T(2,128)}, u32[]{:S(2)}) copy-start(s32[4,2]{0,1:T(2,128)} %param.9) | copy-start | bytes 100
  6.5 508.2 %all-gather.2.cloned.1.call-start = ((), (), s32[]{:S(2)}) async-start(), calls=%async_computation.1 | async-start | bytes 41943040 | tf_op jit(solution)/shard_map/all_gather | solution.py:62
  15.1 9.2 %copy-start.2 = (f32[4,1024]{1,0:T(4,128)S(1)}, f32[4,1024]{1,0:T(4,128)}, u32[]{:S(2)}) copy-start(f32[4,1024]{1,0:T(4,128)} %param.7) | copy-start | bytes 49156
  313.9 1.9 copy-start.3
  634.5 15.2 %copy-start.1 = (s32[4,2]{0,1:T(2,128)S(1)}, s32[4,2]{0,1:T(2,128)}, u32[]{:S(2)}) copy-start(s32[4,2]{0,1:T(2,128)} %param.9) | copy-start | bytes 100
Sparse Core Ops, SparseCore 0:
  314.0 200.6 all-gather.1
where the time goes:
time: 659 us; the launch traced here: 657 us
  waiting for transfers between devices  199 us (30%)
  blocking collectives  190 us (29%)
  local copies, waits for them, and re-layouts  164 us (25%)
  other arithmetic  62.1 us (9%)
  matrix products  26.2 us (4%)
  between operations  14.7 us (2%)
    all_gather x1, waiting for transfers between devices, per_device(): gathered = lax.all_gather(turned, 'bl', axis=0, tiled=True)  199 us
    all_to_all x1, blocking collectives, per_device(): lax.all_to_all(spectra, 'freq', split_axis=3, concat_axis=0, tiled=True)  190 us
    reshape x2, local copies, waits for them, and re-layouts, per_device(): spectra = (spectra * (1.0 / math.sqrt(K))).astype(jnp.bfloat16).reshape(l...  42.6 us
    transpose x3, local copies, waits for them, and re-layouts, arrange(): jnp.transpose(panel, (3, 0, 2, 1))  39.3 us
    reshape x2, local copies, waits for them, and re-layouts, arrange(): jnp.transpose(panel, (3, 0, 2, 1))  28.2 us
    all_to_all x2, local copies, waits for them, and re-layouts, per_device(): lax.all_to_all(spectra, 'freq', split_axis=3, concat_axis=0, tiled=True)  26.3 us
    transpose x3, other arithmetic, arrange(): jnp.transpose(panel, (3, 0, 2, 1))  21.5 us
    convert_element_type x1, other arithmetic, per_device(): filtered = filtered.astype(jnp.bfloat16)  19.3 us
  transfers between devices with their start and end apart: 1, of which 1 were waited for; matrix products, arithmetic and copies ran while one was open for 0% of the time, Pallas kernels for 0%

commit v1 on v0

--- a/solution.py
+++ b/solution.py
@@ -59,7 +59,21 @@
         .reshape(local_count, SAMPLES, 2, K // 2)
     )
     turned = lax.all_to_all(spectra, "freq", split_axis=3, concat_axis=0, tiled=True)
-    gathered = lax.all_gather(turned, "bl", axis=0, tiled=True)
+    ways, here, step = (lax.axis_size("bl"), lax.axis_index("bl"), turned.shape[0])
+    shape = [n * ways if d == 0 else n for d, n in enumerate(turned.shape)]
+    full = lax.dynamic_update_slice_in_dim(
+        jnp.zeros(shape, turned.dtype), turned, here * step, axis=0
+    )
+    going_up = going_down = turned
+    for far in range(1, ways // 2 + 1):
+        going_up = lax.ppermute(going_up, "bl", [(d, (d + 1) % ways) for d in range(ways)])
+        full = lax.dynamic_update_slice_in_dim(full, going_up, (here - far) % ways * step, axis=0)
+        if 2 * far < ways:
+            going_down = lax.ppermute(going_down, "bl", [(d, (d - 1) % ways) for d in range(ways)])
+            full = lax.dynamic_update_slice_in_dim(
+                full, going_down, (here + far) % ways * step, axis=0
+            )
+    gathered = full
     own_tile = tile_list[lax.axis_index("bl")]
     summed = correlate(gathered, antenna_order, own_tile)
     return (summed / SAMPLES).astype(jnp.bfloat16)[None]

time: 659 us -> 738 us (1.12)
  local copies, waits for them, and re-layouts: 164 us -> 219 us
  waiting for transfers between devices: 199 us -> 227 us
  between operations: 14.7 us -> 1.59 us
    ppermute x0 -> x3, waiting for transfers between devices: none -> 227 us  [the longest x2 227 us: per_device(): lax.ppermute(going_up, 'bl', [(d, (d + 1) % ways) for d in range(ways)])]
    all_gather x1 -> x0, waiting for transfers between devices: 199 us -> none  [per_device(): gathered = lax.all_gather(turned, 'bl', axis=0, tiled=True)]
    dynamic_update_slice x0 -> x4, local copies, waits for them, and re-layouts: none -> 42.4 us  [the longest x2 21.2 us: per_device(): lax.dynamic_update_slice_in_dim(full, going_up, (here - far) % ways * ste...]
    broadcast_in_dim x0 -> x1, local copies, waits for them, and re-layouts: none -> 11.3 us  [per_device(): jnp.zeros(shape, turned.dtype)]
  transfers between devices with their start and end apart: 1 -> 3, of which waited for: 1 -> 2; matrix products, arithmetic and copies ran while one was open for 0% -> 6% of each run, Pallas kernels for 0% -> 0%
where the time goes in v1:
time: 738 us; the launch traced here: 729 us
  waiting for transfers between devices  227 us (31%)
  local copies, waits for them, and re-layouts  219 us (30%)
  blocking collectives  190 us (26%)
  other arithmetic  62.1 us (8%)
  matrix products  26.2 us (4%)
    ppermute x2, waiting for transfers between devices, per_device(): lax.ppermute(going_up, 'bl', [(d, (d + 1) % ways) for d in range(ways)])  227 us
    all_to_all x1, blocking collectives, per_device(): lax.all_to_all(spectra, 'freq', split_axis=3, concat_axis=0, tiled=True)  190 us
    reshape x2, local copies, waits for them, and re-layouts, per_device(): spectra = (spectra * (1.0 / math.sqrt(K))).astype(jnp.bfloat16).reshape(l...  42.6 us
    transpose x3, local copies, waits for them, and re-layouts, arrange(): jnp.transpose(panel, (3, 0, 2, 1))  39.2 us
    reshape x2, local copies, waits for them, and re-layouts, arrange(): jnp.transpose(panel, (3, 0, 2, 1))  28.1 us
    all_to_all x2, local copies, waits for them, and re-layouts, per_device(): lax.all_to_all(spectra, 'freq', split_axis=3, concat_axis=0, tiled=True)  26.3 us
    transpose x3, other arithmetic, arrange(): jnp.transpose(panel, (3, 0, 2, 1))  21.5 us
    dynamic_update_slice x2, local copies, waits for them, and re-layouts, per_device(): lax.dynamic_update_slice_in_dim(full, going_up, (here - far) % ways * ste...  21.2 us
  transfers between devices with their start and end apart: 3, of which 2 were waited for; matrix products, arithmetic and copies ran while one was open for 6% of the time, Pallas kernels for 0%

profile of v1, /device:TPU:0, one launch (start us, length us, event | category | flops | bytes accessed | tf_op | source)
XLA Modules:
  0.0 728.5 jit_solution(18148771104185487079)
XLA Ops:
  0.0 0.0 copy-start
  0.0 8.5 %negate_convert_fusion = (bf16[1024,512]{1,0:T(8,128)(2,1)S(1)}, bf16[1024,512]{1,0:T(8,128)(2,1)S(1)}) fusion(), kind=kLoop, calls=%fused_computation.23 | loop fusion | flops 8912896 | bytes 2097152 | tf_op jit(solution)/shard_map/convert.1
  8.6 0.9 fusion.18
  9.4 9.2 %reshape.35 = bf16[32,131,1024]{2,1,0:T(8,128)(2,1)} reshape(bf16[32,134144]{1,0:T(8,128)(2,1)} %param.6) | data formatting | bytes 17170432 | tf_op jit(solution)/shard_map/reshape | solution.py:45
  18.7 19.3 %add_convert_fusion = bf16[32,128,1024]{2,1,0:T(8,128)(2,1)S(1)} fusion(bf16[32,131,1024]{2,1,0:T(8,128)(2,1)} %reshape.35, f32[1024]{0:T(1024)S(1)} %bitcast.30, f32[1024]{0:T(1024)S(1)} %bitcast.31, f32[1024]{0:T(1024)S(1)} %bitcast.29, f32[1024]{0:T(1024)S(1)} %bitcast.28), kind=kLoop, calls=%fused_computation.9 | loop fusion | flops 50331648 | bytes 41959424 | tf_op jit(solution)/shard_map/convert_element_type | solution.py:51
  38.0 11.0 %multiply_convert_fusion.1 = bf16[4096,1024]{1,0:T(8,128)(2,1)} fusion(bf16[4096,1024]{1,0:T(8,128)(2,1)S(1)} %bitcast.26, bf16[1024,512]{1,0:T(8,128)(2,1)S(1)} %get-tuple-element.20, bf16[1024,512]{1,0:T(8,128)(2,1)S(1)} %get-tuple-element.21), kind=kOutput, calls=%fused_computation.8 | convolution fusion | flops 8602517504 | bytes 18874368 | tf_op jit(solution)/shard_map/dot_general | solution.py:53
  48.9 14.5 %reshape.37 = bf16[32,128,2,512]{3,2,1,0:T(2,128)(2,1)} reshape(bf16[4096,1024]{1,0:T(8,128)(2,1)} %multiply_convert_fusion.1) | data formatting | bytes 16777216 | tf_op jit(solution)/shard_map/reshape | solution.py:59
  63.4 28.1 %copy.15 = bf16[32,128,2,512]{1,2,0,3:T(2,128)(2,1)} copy(bf16[32,128,2,512]{3,2,1,0:T(2,128)(2,1)} %reshape.37) | data formatting | bytes 16777216 | tf_op jit(solution)/shard_map/reshape | solution.py:59
  91.5 190.4 %all_to_all.18 = bf16[32,128,2,512]{1,2,0,3:T(2,128)(2,1)} all-to-all(bf16[32,128,2,512]{1,2,0,3:T(2,128)(2,1)} %copy.15), channel_id=1, replica_groups=mesh['freq'=8,'bl'=4] {'freq'}, dimensions={3} | all-to-all | bytes 16777216 | tf_op jit(solution)/shard_map/all_to_all | solution.py:61
  281.9 16.5 %copy.16 = bf16[32,128,2,512]{1,3,2,0:T(8,128)(2,1)} copy(bf16[32,128,2,512]{1,2,0,3:T(2,128)(2,1)} %all_to_all.18) | data formatting | bytes 16777216 | tf_op jit(solution)/shard_map/all_to_all | solution.py:61
  298.4 0.0 copy-start.2
  298.4 9.8 %copy.17 = bf16[8,32,128,2,64]{2,4,3,1,0:T(8,128)(2,1)} copy(bf16[8,32,128,2,64]{2,4,0,3,1:T(8,128)(2,1)} %bitcast.25) | data formatting | bytes 16777216 | tf_op jit(solution)/shard_map/all_to_all | solution.py:61
  308.2 0.0 collective-permute-start
  308.2 1.7 collective-permute-start.1
  309.9 179.4 %collective-permute-done = bf16[256,128,2,64]{1,3,2,0:T(8,128)(2,1)} collective-permute-done((bf16[256,128,2,64]{1,3,2,0:T(8,128)(2,1)}, bf16[256,128,2,64]{1,3,2,0:T(8,128)(2,1)}, u32[]{:S(2)}, u32[]{:S(2)}) %collective-permute-start) | collective-permute-done | bytes 8388640 | tf_op jit(solution)/shard_map/ppermute | solution.py:69
  489.4 0.3 collective-permute-start.2
  489.7 0.0 copy-done
  489.7 0.1 constant_dynamic-slice_fusion
  489.8 0.6 fusion.19
  491.7 0.0 copy-done.2
  491.7 0.1 compare_and_fusion
  491.8 11.3 %broadcast_in_dim.17 = bf16[1024,128,2,64]{1,3,2,0:T(8,128)(2,1)} broadcast(bf16[]{:T(256)} %constant.56.clone.1), dimensions={} | broadcast | bytes 33554432 | tf_op jit(solution)/shard_map/broadcast_in_dim | solution.py:65
  503.0 10.6 %constant_dynamic-update-slice_fusion.3 = bf16[1024,128,2,64]{1,3,2,0:T(8,128)(2,1)} fusion(bf16[1024,128,2,64]{1,3,2,0:T(8,128)(2,1)} %broadcast_in_dim.17, bf16[256,128,2,64]{1,3,2,0:T(8,128)(2,1)} %bitcast.24, s32[]{:T(128)S(6)} %select_n.52), kind=kLoop, calls=%fused_computation.38 | loop fusion | bytes 16777220 | tf_op jit(solution)/shard_map/dynamic_update_slice | solution.py:64
  513.6 10.6 %constant_dynamic-update-slice_fusion.2 = bf16[1024,128,2,64]{1,3,2,0:T(8,128)(2,1)} fusion(bf16[1024,128,2,64]{1,3,2,0:T(8,128)(2,1)} %constant_dynamic-update-slice_fusion.3, bf16[256,128,2,64]{1,3,2,0:T(8,128)(2,1)} %collective-permute-done, s32[]{:T(128)S(6)} %select_n.54), kind=kLoop, calls=%fused_computation.37 | loop fusion | bytes 16777220 | tf_op jit(solution)/shard_map/dynamic_update_slice | solution.py:70
  524.2 0.0 collective-permute-done.1
  524.2 10.6 %constant_dynamic-update-slice_fusion.1 = bf16[1024,128,2,64]{1,3,2,0:T(8,128)(2,1)} fusion(bf16[1024,128,2,64]{1,3,2,0:T(8,128)(2,1)} %constant_dynamic-update-slice_fusion.2, bf16[256,128,2,64]{1,3,2,0:T(8,128)(2,1)} %collective-permute-done.1, s32[]{:T(128)S(6)} %select_n.56), kind=kLoop, calls=%fused_computation.36 | loop fusion | bytes 16777220 | tf_op jit(solution)/shard_map/dynamic_update_slice | solution.py:73
  534.9 47.7 %collective-permute-done.2 = bf16[256,128,2,64]{1,3,2,0:T(8,128)(2,1)} collective-permute-done((bf16[256,128,2,64]{1,3,2,0:T(8,128)(2,1)}, bf16[256,128,2,64]{1,3,2,0:T(8,128)(2,1)}, u32[]{:S(2)}, u32[]{:S(2)}) %collective-permute-start.2) | collective-permute-done | bytes 8388640 | tf_op jit(solution)/shard_map/ppermute | solution.py:69
  582.5 10.6 %constant_dynamic-update-slice_fusion = bf16[1024,128,2,64]{1,3,2,0:T(8,128)(2,1)} fusion(bf16[1024,128,2,64]{1,3,2,0:T(8,128)(2,1)} %constant_dynamic-update-slice_fusion.1, bf16[256,128,2,64]{1,3,2,0:T(8,128)(2,1)} %collective-permute-done.2, s32[]{:T(128)S(6)} %select_n.58), kind=kLoop, calls=%fused_computation.35 | loop fusion | bytes 16777220 | tf_op jit(solution)/shard_map/dynamic_update_slice | solution.py:70
  593.1 9.3 %gather_fusion.1 = bf16[256,128,2,64]{1,3,2,0:T(8,128)(2,1)} fusion(bf16[1024,128,2,64]{1,3,2,0:T(8,128)(2,1)} %constant_dynamic-update-slice_fusion, s32[1024]{0:T(1024)S(1)} %get-tuple-element.22), kind=kCustom, calls=%fused_computation.1.clone | custom fusion | bytes 16778240 | tf_op jit(solution)/shard_map/jit(_take)/gather | solution.py:37
  602.4 7.4 %broadcast_select_fusion = bf16[256,128,2,64]{1,3,2,0:T(8,128)(2,1)} fusion(bf16[256,128,2,64]{1,3,2,0:T(8,128)(2,1)} %gather_fusion.1, pred[256]{0:T(512)(128)(4,1)S(1)} %get-tuple-element.6), kind=kLoop, calls=%fused_computation.12 | loop fusion | flops 4194304 | bytes 16777472 | tf_op jit(solution)/shard_map/jit(_take)/select_n | solution.py:37
  609.9 7.4 %fusion.22 = bf16[64,256,2,128]{3,0,2,1:T(8,128)(2,1)} fusion(bf16[256,128,2,64]{1,3,2,0:T(8,128)(2,1)} %gather_fusion.1, pred[256]{0:T(512)(128)(4,1)S(1)} %get-tuple-element.6), kind=kLoop, calls=%fused_computation.43 | loop fusion | flops 4194304 | bytes 16777472 | tf_op jit(solution)/shard_map/transpose | solution.py:25
  617.3 5.3 slice_negate_fusion
  622.6 6.5 maximum_bitcast_fusion
  629.0 13.2 %copy.20 = bf16[64,256,2,128]{3,2,1,0:T(2,128)(2,1)} copy(bf16[64,256,2,128]{3,0,2,1:T(8,128)(2,1)} %maximum_bitcast_fusion) | data formatting | bytes 16777216 | tf_op jit(solution)/shard_map/transpose | solution.py:25
  642.2 14.0 %reshape.40 = bf16[64,256,256]{2,1,0:T(8,128)(2,1)} reshape(bf16[64,256,2,128]{3,2,1,0:T(2,128)(2,1)} %copy.20) | data formatting | bytes 16777216 | tf_op jit(solution)/shard_map/reshape | solution.py:25
  656.3 13.2 %copy.19 = bf16[64,256,2,128]{3,2,1,0:T(2,128)(2,1)} copy(bf16[64,256,2,128]{3,0,2,1:T(8,128)(2,1)} %fusion.22) | data formatting | bytes 16777216 | tf_op jit(solution)/shard_map/transpose | solution.py:25
  669.4 14.1 %reshape.39 = bf16[64,256,256]{2,1,0:T(8,128)(2,1)} reshape(bf16[64,256,2,128]{3,2,1,0:T(2,128)(2,1)} %copy.19) | data formatting | bytes 16777216 | tf_op jit(solution)/shard_map/reshape | solution.py:25
  683.5 9.1 %gather_fusion = bf16[256,128,2,64]{1,3,2,0:T(8,128)(2,1)} fusion(bf16[1024,128,2,64]{1,3,2,0:T(8,128)(2,1)} %constant_dynamic-update-slice_fusion, s32[1024]{0:T(1024)S(1)} %get-tuple-element.23), kind=kCustom, calls=%fused_computation.clone | custom fusion | bytes 16778240 | tf_op jit(solution)/shard_map/jit(_take)/gather | solution.py:36
  692.6 7.6 %select_bitcast_fusion = bf16[64,256,2,128]{3,0,2,1:T(8,128)(2,1)} fusion(bf16[256,128,2,64]{1,3,2,0:T(8,128)(2,1)} %gather_fusion, pred[256]{0:T(512)(128)(4,1)S(1)} %get-tuple-element.16), kind=kLoop, calls=%fused_computation.11 | loop fusion | flops 4194304 | bytes 16777472 | tf_op jit(solution)/shard_map/transpose | solution.py:25
  700.2 12.9 %copy.18 = bf16[64,256,2,128]{1,3,2,0:T(8,128)(2,1)} copy(bf16[64,256,2,128]{3,0,2,1:T(8,128)(2,1)} %select_bitcast_fusion) | data formatting | bytes 16777216 | tf_op jit(solution)/shard_map/transpose | solution.py:25
  713.1 0.0 copy-start.1
  713.1 15.2 %fusion = bf16[1,64,256,512]{3,2,1,0:T(8,128)(2,1)} fusion(bf16[64,256,256]{1,2,0:T(8,128)(2,1)} %bitcast.27, bf16[64,256,256]{2,1,0:T(8,128)(2,1)} %reshape.40, bf16[64,256,256]{2,1,0:T(8,128)(2,1)} %reshape.39), kind=kOutput, calls=%fused_computation.3 | convolution fusion | flops 4345298944 | bytes 41943040 | tf_op jit(solution)/shard_map/fps,fqs->fpq/dot_general | solution.py:40
  728.3 0.0 copy-done.1
  (1 shorter events, 0.0 us)
Async XLA Ops:
  0.0 489.7 %copy-start = (s32[4,2]{0,1:T(2,128)S(1)}, s32[4,2]{0,1:T(2,128)}, u32[]{:S(2)}) copy-start(s32[4,2]{0,1:T(2,128)} %param.9) | copy-start | bytes 100
  298.4 193.3 %copy-start.2 = (s32[1024]{0:T(1024)S(1)}, s32[1024]{0:T(1024)}, u32[]{:S(2)}) copy-start(s32[1024]{0:T(1024)} %param.8) | copy-start | bytes 12292
  308.2 181.2 %collective-permute-start = (bf16[256,128,2,64]{1,3,2,0:T(8,128)(2,1)}, bf16[256,128,2,64]{1,3,2,0:T(8,128)(2,1)}, u32[]{:S(2)}, u32[]{:S(2)}) collective-permute-start(bf16[256,128,2,64]{1,3,2,0:T(8,128)(2,1)} %bitcast.22), channel_id=1, source_target_pairs={{0,1},{1,2},{2,3},{3,0},{4,5},{5,6},{6,7},{7,4},{8,9},{9,10},{10,1... | collective-permute-start | bytes 25165832 | tf_op jit(solution)/shard_map/ppermute | solution.py:69
  308.2 216.0 %collective-permute-start.1 = (bf16[256,128,2,64]{1,3,2,0:T(8,128)(2,1)}, bf16[256,128,2,64]{1,3,2,0:T(8,128)(2,1)}, u32[]{:S(2)}, u32[]{:S(2)}) collective-permute-start(bf16[256,128,2,64]{1,3,2,0:T(8,128)(2,1)} %bitcast.23), channel_id=1, source_target_pairs={{0,3},{1,0},{2,1},{3,2},{4,7},{5,4},{6,5},{7,6},{8,11},{9,8},{10,9... | collective-permute-start | bytes 25165832 | tf_op jit(solution)/shard_map/ppermute | solution.py:72
  489.4 93.2 %collective-permute-start.2 = (bf16[256,128,2,64]{1,3,2,0:T(8,128)(2,1)}, bf16[256,128,2,64]{1,3,2,0:T(8,128)(2,1)}, u32[]{:S(2)}, u32[]{:S(2)}) collective-permute-start(bf16[256,128,2,64]{1,3,2,0:T(8,128)(2,1)} %collective-permute-done), channel_id=1, source_target_pairs={{0,1},{1,2},{2,3},{3,0},{4,5},{5,6},{6,7},{7,4},{8,9},{9,10},{10,1... | collective-permute-start | bytes 25165832 | tf_op jit(solution)/shard_map/ppermute | solution.py:69
  713.1 15.2 %copy-start.1 = (s32[4,2]{0,1:T(2,128)S(1)}, s32[4,2]{0,1:T(2,128)}, u32[]{:S(2)}) copy-start(s32[4,2]{0,1:T(2,128)} %param.9) | copy-start | bytes 100
